TPU v7x, 512 devices: a whole 4x8x8 slice. The times are simulated.
512 devices in a mesh: dp: 16 (over y, core), frames: 32 (over z, x).
Axes of the slice: x: 4, y: 8, z: 8, core: 2. Of those that a mesh axis runs over, the one named last changes fastest.
Arguments:
- queries: bfloat16 [16, 4096, 2560], P('dp', 'frames'), may hold values from -4.5 to 4.5
- keys: bfloat16 [16, 4096, 2560], P('dp', 'frames'), may hold values from -4.5 to 4.5
- values: bfloat16 [16, 4096, 2560], P('dp', 'frames'), may hold values from -6 to 6
- output_gradient: bfloat16 [16, 4096, 2560], P('dp', 'frames'), as said below
- projection_input: bfloat16 [16, 4096, 5120], P('dp', 'frames'), may hold values from -6 to 6
- blocks: int32 [32, 3, 4, 4], replicated, may hold values from 0 to 1, as said below
- adapter_down_weight: bfloat16 [3, 8, 5120], replicated, may hold values from -0.078125 to 0.078125
- adapter_up_weight: bfloat16 [3, 8, 2560], replicated, may hold values from -2 to 2
Outputs:
- down_grad: float32 [3, 8, 5120], P(None, None, 'frames')
- up_weight_gradient: float32 [3, 8, 2560], P(None, None, 'frames')
Inputs may be any that keep to these rules, and one draw needn't show every extreme that they name: `output_gradient`: every entry lies within 12 / sqrt(65536) of zero. blocks[i, o, a, b] is 1 when query block a of frame i keeps key block b of frame i + o - 1, else 0; every entry with o = 1 is 1; entries naming a frame outside the video are 0.
All inputs are finite; a program needn't handle non-finite values.
Results may differ from a plain program's by a relative error of at most 0.0064.
Values may be sent and summed in bfloat16 or wider, within the bound.
A program may use at most 64 MiB of HBM per device.

v0:
```python
import jax
import jax.numpy as jnp
from jax import lax
from jax.sharding import PartitionSpec as P

HEAD_WIDTH = 128
REACH = 1


ADAPTER_SCALE = 2.0


def shifted(block, axis, distance):
    devices = range(lax.axis_size(axis))
    route = [(i - distance, i) for i in devices if i - distance in devices]
    return lax.ppermute(block, axis, route)


def grow_table(block_table, length):
    block_rows = length // block_table.shape[-1]
    grown = jnp.repeat(jnp.repeat(block_table, block_rows, axis=-2), block_rows, axis=-1)
    return grown > 0


def per_device(
    queries,
    keys,
    values,
    output_gradient,
    projection_input,
    blocks,
    adapter_down_weight,
    adapter_up_weight,
):
    tokens = queries.shape[1]
    row_width = queries.shape[2]
    head_count = row_width // HEAD_WIDTH
    score_scale = HEAD_WIDTH ** (-0.5)
    my_frame = lax.axis_index("frames")
    offsets = list(range(-REACH, REACH + 1))
    far_offsets = [offset for offset in offsets if offset != 0]
    centre = REACH
    own_query = queries[0]
    own_key = keys[0]
    own_value = values[0]
    own_grad = output_gradient[0]
    own_table = lax.dynamic_index_in_dim(blocks, my_frame, 0, keepdims=False)
    allowed = jnp.transpose(grow_table(own_table, tokens), (1, 0, 2))
    arrived = {}
    for offset in far_offsets:
        arrived[offset] = shifted((own_key, own_value), "frames", offset)
    key_list = [own_key if offset == 0 else arrived[-offset][0] for offset in offsets]
    value_list = [own_value if offset == 0 else arrived[-offset][1] for offset in offsets]
    key_stack = jnp.stack(key_list).reshape(len(offsets), tokens, head_count, HEAD_WIDTH)
    value_stack = jnp.stack(value_list).reshape(len(offsets), tokens, head_count, HEAD_WIDTH)
    query_shaped = own_query.reshape(tokens, head_count, HEAD_WIDTH)
    grad_shaped = own_grad.reshape(tokens, head_count, HEAD_WIDTH)
    scores = (
        jnp.einsum("thd,oshd->htos", query_shaped, key_stack, preferred_element_type=jnp.float32)
        * score_scale
    )
    masked = jnp.where(allowed[None], scores, -jnp.inf)
    row_top = jnp.max(masked, axis=(2, 3))
    row_total = jnp.sum(jnp.exp(masked - row_top[:, :, None, None]), axis=(2, 3))
    log_total = row_top + jnp.log(row_total)
    weights = jnp.exp(masked - log_total[:, :, None, None])
    weight_grads = jnp.einsum(
        "thd,oshd->htos", grad_shaped, value_stack, preferred_element_type=jnp.float32
    )
    row_delta = jnp.sum(weights * weight_grads, axis=(2, 3))
    score_grads = (weights * (weight_grads - row_delta[:, :, None, None])).astype(jnp.bfloat16)
    low_weights = weights.astype(jnp.bfloat16)
    grad_q = (
        jnp.einsum("htos,oshd->thd", score_grads, key_stack, preferred_element_type=jnp.float32)
        * score_scale
    ).astype(jnp.bfloat16)
    grad_q = grad_q.reshape(tokens, row_width)
    key_part = (
        jnp.einsum("htos,thd->oshd", score_grads, query_shaped, preferred_element_type=jnp.float32)
        * score_scale
    )
    value_part = jnp.einsum(
        "htos,thd->oshd", low_weights, grad_shaped, preferred_element_type=jnp.float32
    )
    key_part = key_part.reshape(len(offsets), tokens, row_width)
    value_part = value_part.reshape(len(offsets), tokens, row_width)
    key_total = key_part[centre]
    value_total = value_part[centre]
    for position, offset in enumerate(offsets):
        if offset != 0:
            returned = shifted((key_part[position], value_part[position]), "frames", offset)
            key_total = key_total + returned[0]
            value_total = value_total + returned[1]
    grad_k = key_total.astype(jnp.bfloat16)
    grad_v = value_total.astype(jnp.bfloat16)
    gradient_list = jnp.stack([grad_q, grad_k, grad_v])
    hidden_state = projection_input[0]
    reduced_activation = jnp.einsum(
        "vi,hui->hvu", hidden_state, adapter_down_weight, preferred_element_type=jnp.float32
    ).astype(jnp.bfloat16)
    middle_activation = (
        ADAPTER_SCALE
        * jnp.einsum(
            "smj,sgj->smg", gradient_list, adapter_up_weight, preferred_element_type=jnp.float32
        )
    ).astype(jnp.bfloat16)
    up_weight_gradient = ADAPTER_SCALE * jnp.einsum(
        "giq,gim->gqm", reduced_activation, gradient_list, preferred_element_type=jnp.float32
    )
    down_grad = jnp.einsum(
        "ctr,td->crd", middle_activation, hidden_state, preferred_element_type=jnp.float32
    )
    down_shard, up_shard = (
        lax.psum_scatter(down_grad, "frames", scatter_dimension=2, tiled=True),
        lax.psum_scatter(up_weight_gradient, "frames", scatter_dimension=2, tiled=True),
    )
    down_shard, up_shard = lax.psum((down_shard, up_shard), "dp")
    return (down_shard, up_shard)


def solution(mesh):
    return jax.shard_map(
        per_device,
        mesh=mesh,
        in_specs=(
            P("dp", "frames", None),
            P("dp", "frames", None),
            P("dp", "frames", None),
            P("dp", "frames", None),
            P("dp", "frames", None),
            P(),
            P(),
            P(),
        ),
        out_specs=(P(None, None, "frames"), P(None, None, "frames")),
        check_vma=False,
    )
```

profile of v0, /device:TPU:1, one launch (start us, length us, event | category | flops | bytes accessed | tf_op | source)
XLA Modules:
  0.0 656.1 jit_solution(2208405619092323852)
XLA Ops:
  10.9 5.4 collective-permute-start.2
  19.8 4.9 collective-permute-start
  34.0 3.5 collective-permute-done.1
  41.9 2.4 fusion.36
  50.8 2.9 copy.74
  53.6 2.8 copy.75
  56.4 2.9 copy.77
  59.3 2.8 copy.78
  62.1 9.0 %collective-permute-start.5 = (f32[128,2560]{1,0:T(8,128)}, f32[128,2560]{1,0:T(8,128)}, u32[]{:S(2)}, u32[]{:S(2)}) collective-permute-start(f32[128,2560]{1,0:T(8,128)} %copy.78), channel_id=1, source_target_pairs={{0,1},{1,2},{2,3},{3,4},{4,5},{5,6},{6,7},{7,8},{8,9},{9,10},{10,1... | collective-permute-start | bytes 3932168 | tf_op jit(solution)/shard_map/ppermute | solution.py:16
  72.4 3.2 convolution_bitcast_fusion
  77.6 2.8 copy.80
  80.4 2.8 copy.82
  83.2 5.0 collective-permute-start.7
  89.7 3.2 fusion.13
  99.1 2.6 collective-permute-done.4
  104.1 20.8 %collective-permute-done.7 = f32[128,2560]{1,0:T(8,128)} collective-permute-done((f32[128,2560]{1,0:T(8,128)}, f32[128,2560]{1,0:T(8,128)}, u32[]{:S(2)}, u32[]{:S(2)}) %collective-permute-start.7) | collective-permute-done | bytes 1310752 | tf_op jit(solution)/shard_map/ppermute | solution.py:16
  124.9 5.0 collective-permute-done.6
  134.0 3.5 copy.101
  137.5 6.0 reshape.55
  145.6 7.7 %copy.99 = f32[3,8,5120]{1,0,2:T(4,128)} copy(f32[3,8,5120]{2,1,0:T(8,128)} %fusion.16) | data formatting | bytes 983040
  153.3 10.9 %reshape.53 = f32[5120,24]{1,0:T(8,128)} reshape(f32[5120,3,8]{2,1,0:T(4,128)} %bitcast.87) | data formatting | bytes 983040
  164.2 208.5 %reduce-scatter.9.cloned.1.call-done = f32[80,24]{1,0:T(8,128)} async-done(((f32[2560,24]{1,0:T(8,128)}), f32[80,24]{1,0:T(8,128)}) %reduce-scatter.9.cloned.1.call-update) | async-done | bytes 7696
  373.7 225.7 %reduce-scatter.7.cloned.1.call-done = f32[160,24]{1,0:T(8,128)} async-done(((f32[5120,24]{1,0:T(8,128)}), f32[160,24]{1,0:T(8,128)}) %reduce-scatter.7.cloned.1.call-update) | async-done | bytes 15376
  600.6 48.7 %all-reduce = (f32[3,8,160]{2,1,0:T(8,128)}, f32[3,8,80]{2,1,0:T(8,128)}) all-reduce(f32[3,8,160]{2,1,0:T(8,128)S(1)} %copy.100, f32[3,8,80]{2,1,0:T(8,128)S(1)} %copy.102), channel_id=1, replica_groups=mesh['dp'=16,'frames'=32] {'dp'}, use_global_device_ids=true, to_apply=%region_4.5 | all-reduce | flops 5760 | bytes 46080 | tf_op jit(solution)/shard_map/psum | solution.py:117
  (68 shorter events, 48.9 us)
Async XLA Ops:
  7.2 124.7 %copy-start = (bf16[1,128,5120]{2,1,0:T(8,128)(2,1)S(1)}, bf16[1,128,5120]{2,1,0:T(8,128)(2,1)}, u32[]{:S(2)}) copy-start(bf16[1,128,5120]{2,1,0:T(8,128)(2,1)} %param.12) | copy-start | bytes 3932164
  7.2 17.5 %copy-start.9 = (s32[32,3,4,4]{0,3,2,1:T(4,128)S(1)}, s32[32,3,4,4]{0,3,2,1:T(4,128)}, u32[]{:S(2)}) copy-start(s32[32,3,4,4]{0,3,2,1:T(4,128)} %param.13) | copy-start | bytes 18436
  7.2 365.5 %reduce-scatter.9.cloned.1.call-start = ((), (), s32[]{:S(2)}) async-start(), calls=%async_computation.3 | async-start | bytes 1351680
  9.5 19.3 %copy-start.7 = (bf16[1,128,2560]{2,1,0:T(8,128)(2,1)S(1)}, bf16[1,128,2560]{2,1,0:T(8,128)(2,1)}, u32[]{:S(2)}) copy-start(bf16[1,128,2560]{2,1,0:T(8,128)(2,1)} %param.8) | copy-start | bytes 1966084
  9.5 20.7 %collective-permute-start.3 = (bf16[128,2560]{0,1:T(8,128)(2,1)}, bf16[128,2560]{0,1:T(8,128)(2,1)}, u32[]{:S(2)}, u32[]{:S(2)}) collective-permute-start(bf16[128,2560]{0,1:T(8,128)(2,1)} %bitcast.10), channel_id=1, source_target_pairs={{1,0},{2,1},{3,2},{4,3},{5,4},{6,5},{7,6},{8,7},{9,8},{10,9},{11,1... | collective-permute-start | bytes 1966088 | tf_op jit(solution)/shard_map/ppermute | solution.py:16
  10.9 20.9 %collective-permute-start.2 = (bf16[128,2560]{0,1:T(8,128)(2,1)}, bf16[128,2560]{0,1:T(8,128)(2,1)}, u32[]{:S(2)}, u32[]{:S(2)}) collective-permute-start(bf16[128,2560]{0,1:T(8,128)(2,1)} %bitcast.10), channel_id=1, source_target_pairs={{0,1},{1,2},{2,3},{3,4},{4,5},{5,6},{6,7},{7,8},{8,9},{9,10},{10,1... | collective-permute-start | bytes 1966088 | tf_op jit(solution)/shard_map/ppermute | solution.py:16
  18.5 19.0 %collective-permute-start.1 = (bf16[128,2560]{0,1:T(8,128)(2,1)}, bf16[128,2560]{0,1:T(8,128)(2,1)}, u32[]{:S(2)}, u32[]{:S(2)}) collective-permute-start(bf16[128,2560]{0,1:T(8,128)(2,1)} %bitcast), channel_id=1, source_target_pairs={{1,0},{2,1},{3,2},{4,3},{5,4},{6,5},{7,6},{8,7},{9,8},{10,9},{11,1... | collective-permute-start | bytes 1966088 | tf_op jit(solution)/shard_map/ppermute | solution.py:16
  19.8 19.9 %collective-permute-start = (bf16[128,2560]{0,1:T(8,128)(2,1)}, bf16[128,2560]{0,1:T(8,128)(2,1)}, u32[]{:S(2)}, u32[]{:S(2)}) collective-permute-start(bf16[128,2560]{0,1:T(8,128)(2,1)} %bitcast), channel_id=1, source_target_pairs={{0,1},{1,2},{2,3},{3,4},{4,5},{5,6},{6,7},{7,8},{8,9},{9,10},{10,1... | collective-permute-start | bytes 1966088 | tf_op jit(solution)/shard_map/ppermute | solution.py:16
  25.1 4.7 copy-start.8
  30.2 14.8 %copy-start.2 = (bf16[1,128,2560]{1,2,0:T(8,128)(2,1)}, bf16[1,128,2560]{1,2,0:T(8,128)(2,1)S(1)}, u32[]{:S(2)}) copy-start(bf16[1,128,2560]{1,2,0:T(8,128)(2,1)S(1)} %copy.67) | copy-start | bytes 1966084
  44.4 2.6 copy-start.1
  44.4 1.6 copy-start.5
  47.0 1.1 copy-start.6
  62.1 37.1 %collective-permute-start.5 = (f32[128,2560]{1,0:T(8,128)}, f32[128,2560]{1,0:T(8,128)}, u32[]{:S(2)}, u32[]{:S(2)}) collective-permute-start(f32[128,2560]{1,0:T(8,128)} %copy.78), channel_id=1, source_target_pairs={{0,1},{1,2},{2,3},{3,4},{4,5},{5,6},{6,7},{7,8},{8,9},{9,10},{10,1... | collective-permute-start | bytes 3932168 | tf_op jit(solution)/shard_map/ppermute | solution.py:16
  71.1 30.7 %collective-permute-start.4 = (f32[128,2560]{1,0:T(8,128)}, f32[128,2560]{1,0:T(8,128)}, u32[]{:S(2)}, u32[]{:S(2)}) collective-permute-start(f32[128,2560]{1,0:T(8,128)} %copy.75), channel_id=1, source_target_pairs={{1,0},{2,1},{3,2},{4,3},{5,4},{6,5},{7,6},{8,7},{9,8},{10,9},{11,1... | collective-permute-start | bytes 3932168 | tf_op jit(solution)/shard_map/ppermute | solution.py:16
  83.2 41.7 %collective-permute-start.7 = (f32[128,2560]{1,0:T(8,128)}, f32[128,2560]{1,0:T(8,128)}, u32[]{:S(2)}, u32[]{:S(2)}) collective-permute-start(f32[128,2560]{1,0:T(8,128)} %copy.82), channel_id=1, source_target_pairs={{0,1},{1,2},{2,3},{3,4},{4,5},{5,6},{6,7},{7,8},{8,9},{9,10},{10,1... | collective-permute-start | bytes 3932168 | tf_op jit(solution)/shard_map/ppermute | solution.py:16
  88.3 41.6 %collective-permute-start.6 = (f32[128,2560]{1,0:T(8,128)}, f32[128,2560]{1,0:T(8,128)}, u32[]{:S(2)}, u32[]{:S(2)}) collective-permute-start(f32[128,2560]{1,0:T(8,128)} %copy.80), channel_id=1, source_target_pairs={{1,0},{2,1},{3,2},{4,3},{5,4},{6,5},{7,6},{8,7},{9,8},{10,9},{11,1... | collective-permute-start | bytes 3932168 | tf_op jit(solution)/shard_map/ppermute | solution.py:16
  92.9 1.5 copy-start.4
  99.1 30.7 %copy-start.3 = (f32[128,2560]{1,0:T(8,128)S(1)}, f32[128,2560]{1,0:T(8,128)}, u32[]{:S(2)}) copy-start(f32[128,2560]{1,0:T(8,128)} %copy.81) | copy-start | bytes 3932164
  137.5 6.1 copy-start.10
  143.6 455.8 %reduce-scatter.7.cloned.1.call-start = ((), (), s32[]{:S(2)}) async-start(), calls=%async_computation.2 | async-start | bytes 2703360
Sparse Core Ops, SparseCore 0:
  143.7 228.9 reduce-scatter.8
  377.1 222.2 reduce-scatter.6
where the time goes:
time: 660 us; the launch traced here: 656 us
  waiting for transfers between devices  466 us (71%)
  local copies, waits for them, and re-layouts  76.3 us (12%)
  blocking collectives  48.7 us (7%)
  starting transfers between devices  29.9 us (5%)
  matrix products  14.8 us (2%)
  between operations  14.3 us (2%)
    unnamed x4, waiting for transfers between devices  434 us
    psum x1, blocking collectives, per_device(): down_shard, up_shard = lax.psum((down_shard, up_shard), 'dp')  48.7 us
    unnamed x34, local copies, waits for them, and re-layouts  37.1 us
    ppermute x8, waiting for transfers between devices, shifted(): return lax.ppermute(block, axis, route)  31.9 us
    ppermute x8, starting transfers between devices, shifted(): return lax.ppermute(block, axis, route)  29.8 us
  transfers between devices with their start and end apart: 10, of which 6 were waited for; matrix products, arithmetic and copies ran while one was open for 9% of the time, Pallas kernels for 0%

commit v1 on v0

v1 whole, which is shorter than its diff:
```python
import functools
import math

import jax
import jax.numpy as jnp
from jax import lax
from jax.experimental import pallas as pl
from jax.experimental.pallas import tpu as pltpu
from jax.sharding import PartitionSpec as P

HEAD = 128
RANK = 8
ADAPTER_SCALE = 2.0
MASKED = -1e30
CHIPS_X = 4
MESH = pl.DeviceIdType.MESH
BF16 = jnp.bfloat16
F32 = jnp.float32
NT = (((1,), (1,)), ((), ()))
NN = (((1,), (0,)), ((), ()))
TN = (((0,), (0,)), ((), ()))


def dot(a, b, dims=NN):
    return lax.dot_general(a, b, dims, preferred_element_type=F32)


def kernel(cfg, q_hbm, k_hbm, v_hbm, g_hbm, x_hbm, blocks_hbm, a_hbm, u_hbm, down_out, up_out, *scratch):
    (qb, gb, kb, vb, xb, ab, ub, bb, bias, lowb, lowq, uall, gqb, gkb, gvb, midq, midkv, mrx, db, upb, st,
     cbuf, crx, xsb, xrx, zb, zf, zrx, ysb, yrx, fb,
     local_sem, ks_sem, kr_sem, ls_sem, lr_sem, ms_sem, mr_sem, cs_sem, cr_sem, xs_sem, xr_sem, zs_sem, zr_sem,
     ys_sem, yr_sem, fs_sem, fr_sem) = scratch
    frames, dps, chunks, chunk, window, up_width, lag = cfg
    X, Y = CHIPS_X, dps // 2
    Z = frames // X
    width, model = qb.shape[1], xb.shape[1]
    tokens = qb.shape[0]
    span = 3 * tokens
    dp = lax.axis_index("dp")
    frame = lax.axis_index("frames")
    y, core = dp // 2, dp % 2
    z, x = frame // X, frame % X
    sibling = (y * 2 + 1 - core, frame)
    halo = [(dp, (frame + 1) % frames), (dp, (frame + frames - 1) % frames)]
    xs = [(dp, z * X + (x + d) % X) for d in range(1, X)]
    zs = [(dp, ((z + d) % Z) * X + x) for d in range(1, Z)]
    ys = [(((y + d) % Y) * 2 + core, frame) for d in range(1, Y)]

    local = [
        pltpu.make_async_copy(src, dst, local_sem.at[i])
        for i, (src, dst) in enumerate([
            (q_hbm.at[0], qb), (k_hbm.at[0], kb.at[1]), (v_hbm.at[0], vb.at[1]), (g_hbm.at[0], gb),
            (x_hbm.at[0], xb), (a_hbm, ab), (u_hbm, ub), (blocks_hbm.at[frame], bb),
        ])
    ]
    for copy in local:
        copy.start()
    everyone = halo + xs + zs + ys + [sibling]
    barrier = pltpu.get_barrier_semaphore()
    for peer in everyone:
        pl.semaphore_signal(barrier, inc=1, device_id=peer, device_id_type=MESH)
    pl.semaphore_wait(barrier, len(everyone))

    def remote(src, dst, send, recv, peer):
        return pltpu.make_async_remote_copy(
            src_ref=src, dst_ref=dst, send_sem=send, recv_sem=recv, device_id=peer, device_id_type=MESH)

    def halo_copy(c, side, kind):
        cols = pl.ds(pl.multiple_of(c * chunk, 128), chunk)
        src, dst = ((k_hbm, kb), (v_hbm, vb))[kind]
        return remote(src.at[0, :, cols], dst.at[2 * side, :, cols],
                      ks_sem.at[side, kind, c], kr_sem.at[side, kind, c], halo[side])

    def halo_start(c):
        for kind in range(2):
            for side in range(2):
                halo_copy(c, side, kind).start()

    @pl.loop(0, window)
    def _(c):
        halo_start(c)

    local[7].wait()
    lane_block = lax.broadcasted_iota(jnp.int32, (1, tokens), 1) // (tokens // 4)
    for o in range(3):
        table = bb[o]
        for b in range(4):
            row = jnp.zeros((1, tokens), jnp.int32)
            for a in range(4):
                row = jnp.where(lane_block == a, jnp.broadcast_to(table[a:a + 1, b:b + 1], (1, tokens)), row)
            line = jnp.where(row > 0, 0.0, MASKED).astype(F32)
            bias[pl.ds(o * tokens + b * (tokens // 4), tokens // 4), :] = jnp.broadcast_to(line, (tokens // 4, tokens))

    local[6].wait()
    uall[...] = jnp.concatenate([ub[1].astype(F32), ub[2].astype(F32), ub[0].astype(F32), ub[0].astype(F32)], 0).astype(BF16)
    local[5].wait()
    local[4].wait()
    stacked = jnp.concatenate([ab[1].astype(F32), ab[2].astype(F32), ab[0].astype(F32), ab[0].astype(F32)], 0).astype(BF16)
    low = dot(stacked, xb[...], NT).astype(BF16)
    lowb[1] = low[0:2 * RANK]
    lowq[...] = low[2 * RANK:4 * RANK]
    low_copies = [remote(lowb.at[1], lowb.at[2 * side], ls_sem.at[side], lr_sem.at[side], halo[side]) for side in range(2)]
    for copy in low_copies:
        copy.start()
    midq[...] = jnp.zeros_like(midq)
    midkv[...] = jnp.zeros_like(midkv)
    upb[...] = jnp.zeros_like(upb)
    for i in range(4):
        local[i].wait()

    def up_step(p):
        cols = pl.ds(pl.multiple_of(p * up_width, 128), up_width)
        lows = jnp.concatenate([lowb[0], lowb[1], lowb[2]], 1)
        upb[0:RANK, cols] = ADAPTER_SCALE * dot(lows, gkb[:, cols])[0:RANK]
        upb[RANK:2 * RANK, cols] = ADAPTER_SCALE * dot(lows, gvb[:, cols])[RANK:2 * RANK]
        upb[2 * RANK:3 * RANK, cols] = ADAPTER_SCALE * dot(lowq[...], gqb[:, cols])[0:RANK]

    scale = HEAD ** -0.5
    scale2 = scale * math.log2(math.e)
    steps_inside = len([c for c in range(lag, chunks) if (c - lag + 1) * up_width <= c * chunk])

    @pl.loop(0, chunks)
    def _(c):
        for kind in range(2):
            for side in range(2):
                halo_copy(c, side, kind).wait()

        @pl.when(c + window < chunks)
        def _():
            halo_start(c + window)

        @pl.when(c == lag)
        def _():
            for copy in low_copies:
                copy.wait()

        @pl.when((c >= lag) & (c < lag + steps_inside))
        def _():
            up_step(c - lag)

        for h in range(chunk // HEAD):
            cols = pl.ds(pl.multiple_of(c * chunk + h * HEAD, 128), HEAD)
            q, g = qb[:, cols], gb[:, cols]
            kc = kb[:, :, cols].reshape(span, HEAD)
            vc = vb[:, :, cols].reshape(span, HEAD)
            s = dot(kc, q, NT) * scale2 + bias[...]
            e = jnp.exp2(s - jnp.max(s, axis=0, keepdims=True))
            w = e * (1.0 / jnp.sum(e, axis=0, keepdims=True))
            wg = dot(vc, g, NT)
            delta = jnp.sum(w * wg, axis=0, keepdims=True)
            ds = (w * (wg - delta)).astype(BF16)
            gkb[:, cols] = (dot(ds, q) * scale).astype(BF16)
            gvb[:, cols] = dot(w.astype(BF16), g).astype(BF16)
            gqb[:, cols] = (dot(ds, kc, TN) * scale).astype(BF16)
        cols = pl.ds(pl.multiple_of(c * chunk, 128), chunk)
        ukv, uq = uall[0:2 * RANK, cols], uall[2 * RANK:4 * RANK, cols]
        mk = dot(ukv, gkb[:, cols], NT)
        mv = dot(ukv, gvb[:, cols], NT)
        midq[...] += dot(uq, gqb[:, cols], NT)[0:RANK]
        for o in range(3):
            part = slice(o * tokens, (o + 1) * tokens)
            midkv[o] += jnp.concatenate([mk[0:RANK, part], mv[RANK:2 * RANK, part]], 0)

    mid_copies = [remote(midkv.at[2 - 2 * side], mrx.at[side], ms_sem.at[side], mr_sem.at[side], halo[side]) for side in range(2)]
    for copy in mid_copies:
        copy.start()
    for p in range(steps_inside, width // up_width):
        up_step(p)
    for copy in mid_copies:
        copy.wait_recv()
    mid = (ADAPTER_SCALE * jnp.concatenate([midkv[1] + mrx[0] + mrx[1], midq[...]], 0)).astype(BF16)
    db[...] = dot(mid, xb[...])

    down_block, up_block = model // frames, width // frames
    rows = 3 * RANK
    lane = lax.broadcasted_iota(jnp.int32, (rows, 128), 1)

    @pl.loop(0, Z // 2)
    def _(pair):
        for j in range(2 * X):
            down_base = pl.multiple_of(pair * (2 * X * down_block), 128)
            up_base = pl.multiple_of(pair * (2 * X * up_block), 128)
            at = down_block * j
            first = db[:, pl.ds(down_base + at // 128 * 128, 256)]
            first = pltpu.roll(first, (256 - at % 128) % 256, 1)[:, 0:128]
            at += 128
            second = db[:, pl.ds(down_base + at // 128 * 128, 128)]
            second = pltpu.roll(second, (128 - at % 128) % 128, 1)
            at = up_block * j
            third = upb[:, pl.ds(up_base + at // 128 * 128, 256)]
            third = pltpu.roll(third, (256 + 32 - at % 128) % 256, 1)[:, 0:128]
            place = pl.ds(pl.multiple_of((2 * pair + j // X) * rows, 8), rows)
            st[0, j % X, place, :] = first
            st[1, j % X, place, :] = jnp.where(lane < 32, second, jnp.where(lane < 32 + up_block, third, 0.0))

    turn = [(x + 1 + i) % X for i in range(X)]
    core_copies = [remote(cbuf.at[i], crx.at[i], cs_sem.at[i], cr_sem.at[i], sibling) for i in range(X)]
    for i in range(X):
        cbuf[i] = st[1 - core, turn[i]].astype(BF16)
        core_copies[i].start()
    x_copies = [remote(xsb.at[i], xrx.at[i], xs_sem.at[i], xr_sem.at[i], xs[i]) for i in range(X - 1)]
    for i in range(X - 1):
        core_copies[i].wait_recv()
        xsb[i] = (st[core, turn[i]] + crx[i].astype(F32)).astype(BF16)
        x_copies[i].start()
    core_copies[X - 1].wait_recv()
    total = st[core, x] + crx[X - 1].astype(F32)
    for i in range(X - 1):
        x_copies[i].wait_recv()
        total = total + xrx[i].astype(F32)
    total = total.reshape(Z, rows, 128)
    zf[...] = total
    zb[...] = jnp.concatenate([total, jnp.zeros((Z, 32 - rows, 128), F32)], 1).astype(BF16)
    z_copies = [remote(zb.at[(z + 1 + i) % Z], zrx.at[i], zs_sem.at[i], zr_sem.at[i], zs[i]) for i in range(Z - 1)]
    for copy in z_copies:
        copy.start()
    total = zf[z]
    for i in range(Z - 1):
        z_copies[i].wait_recv()
        total = total + zrx[i].astype(F32)[0:rows]
    mine = jnp.concatenate([total, jnp.zeros((32 - rows, 128), F32)], 0).astype(BF16)
    ysb[...] = mine
    y_copies = [remote(ysb, yrx.at[y], ys_sem.at[i], yr_sem.at[i], ys[i]) for i in range(Y - 1)]
    for copy in y_copies:
        copy.start()
    yrx[y] = mine
    for copy in y_copies:
        copy.wait_recv()
    total = yrx[0].astype(F32)
    for i in range(1, Y):
        total = total + yrx[i].astype(F32)
    fb[core] = total[0:rows]
    last = remote(fb.at[core], fb.at[core], fs_sem, fr_sem, sibling)
    last.start()
    last.wait_recv()
    left, right = fb[0], fb[1]
    shifted = pltpu.roll(right, 128 - 32, 1)
    for place, c in enumerate((1, 2, 0)):
        part = slice(place * RANK, (place + 1) * RANK)
        down_out[c, :, 0:128] = left[part]
        down_out[c, :, 128:down_block] = right[part, 0:down_block - 128]
        up_out[c] = shifted[part, 0:up_block]
    for copy in mid_copies + core_copies + x_copies + z_copies + y_copies + [last]:
        copy.wait_send()


def per_device(frames, dps, q, k, v, g, x, blocks, a, u):
    tokens, width = q.shape[1:]
    model = x.shape[2]
    heads = width // HEAD
    per_chunk = 2 if heads % 4 == 0 else 1
    chunk = per_chunk * HEAD
    chunks = heads // per_chunk
    window = min(4, chunks)
    up_width = 2 * chunk if heads % 4 == 0 else chunk
    lag = chunks // 2 if heads % 4 == 0 else 3
    Y, Z, X = dps // 2, frames // CHIPS_X, CHIPS_X
    rows = 3 * RANK
    vmem = pltpu.VMEM
    dma = pltpu.SemaphoreType.DMA
    scratch = [
        vmem((tokens, width), BF16), vmem((tokens, width), BF16),
        vmem((3, tokens, width), BF16), vmem((3, tokens, width), BF16),
        vmem((tokens, model), BF16), vmem((3, RANK, model), BF16), vmem((3, RANK, width), BF16),
        vmem((3, 4, 4), jnp.int32), vmem((3 * tokens, tokens), F32),
        vmem((3, 2 * RANK, tokens), BF16), vmem((2 * RANK, tokens), BF16), vmem((4 * RANK, width), BF16),
        vmem((tokens, width), BF16), vmem((3 * tokens, width), BF16), vmem((3 * tokens, width), BF16),
        vmem((RANK, tokens), F32), vmem((3, 2 * RANK, tokens), F32), vmem((2, 2 * RANK, tokens), F32),
        vmem((rows, model), F32), vmem((rows, width + 128), F32), vmem((2, X, Z * rows, 128), F32),
        vmem((X, Z * rows, 128), BF16), vmem((X, Z * rows, 128), BF16),
        vmem((X - 1, Z * rows, 128), BF16), vmem((X - 1, Z * rows, 128), BF16),
        vmem((Z, 32, 128), BF16), vmem((Z, rows, 128), F32), vmem((max(Z - 1, 1), 32, 128), BF16),
        vmem((32, 128), BF16), vmem((Y, 32, 128), BF16), vmem((2, rows, 128), F32),
        dma((8,)), dma((2, 2, chunks)), dma((2, 2, chunks)), dma((2,)), dma((2,)), dma((2,)), dma((2,)),
        dma((X,)), dma((X,)), dma((X - 1,)), dma((X - 1,)), dma((max(Z - 1, 1),)), dma((max(Z - 1, 1),)),
        dma((max(Y - 1, 1),)), dma((max(Y - 1, 1),)), dma, dma,
    ]
    return pl.pallas_call(
        functools.partial(kernel, (frames, dps, chunks, chunk, window, up_width, lag)),
        out_shape=(
            jax.ShapeDtypeStruct((3, RANK, model // frames), F32),
            jax.ShapeDtypeStruct((3, RANK, width // frames), F32),
        ),
        in_specs=[pl.BlockSpec(memory_space=pltpu.HBM)] * 8,
        out_specs=(pl.BlockSpec(memory_space=pltpu.VMEM), pl.BlockSpec(memory_space=pltpu.VMEM)),
        scratch_shapes=scratch,
        compiler_params=pltpu.CompilerParams(collective_id=0, has_side_effects=True, vmem_limit_bytes=48 << 20),
    )(q, k, v, g, x, blocks, a, u)


def solution(mesh):
    split = P("dp", "frames", None)
    return jax.shard_map(
        functools.partial(per_device, mesh.shape["frames"], mesh.shape["dp"]),
        mesh=mesh,
        in_specs=(split,) * 5 + (P(), P(), P()),
        out_specs=(P(None, None, "frames"), P(None, None, "frames")),
        check_vma=False,
    )
```

time: 660 us -> 81.6 us (0.12)
  waiting for transfers between devices: 466 us -> 0 us
  Pallas kernels: 0 us -> 70.9 us
  local copies, waits for them, and re-layouts: 76.3 us -> 9.61 us
  blocking collectives: 48.7 us -> 0 us
  starting transfers between devices: 29.9 us -> 0 us
  matrix products: 14.8 us -> 0 us
  between operations: 14.3 us -> 0.66 us
    unnamed x4 -> x0, waiting for transfers between devices: 434 us -> none
    pallas_call x0 -> x1, Pallas kernels: none -> 70.9 us  [per_device(): pl.pallas_call(functools.partial(kernel, (frames, dps, chunks, chunk, win...]
    psum x1 -> x0, blocking collectives: 48.7 us -> none  [per_device(): down_shard, up_shard = lax.psum((down_shard, up_shard), 'dp')]
    ppermute x8 -> x0, waiting for transfers between devices: 31.9 us -> none  [shifted(): return lax.ppermute(block, axis, route)]
    ppermute x8 -> x0, starting transfers between devices: 29.8 us -> none  [shifted(): return lax.ppermute(block, axis, route)]
    unnamed x34 -> x17, local copies, waits for them, and re-layouts: 37.1 us -> 9.61 us
    dot_general x7 -> x0, matrix products: 14.8 us -> none  [the longest x1 3.23 us: per_device(): jnp.einsum('htos,thd->oshd', low_weights, grad_shaped, preferred_element_...]
    squeeze x6 -> x0, local copies, waits for them, and re-layouts: 14.2 us -> none  [the longest x2 5.6 us: per_device(): value_part[position]]
  transfers between devices with their start and end apart: 10 -> 0, of which waited for: 6 -> 0; matrix products, arithmetic and copies ran while one was open for 9% -> 0% of each run, Pallas kernels for 0% -> 0%
where the time goes in v1:
time: 81.6 us; the launch traced here: 81.2 us
  Pallas kernels  70.9 us (87%)
  local copies, waits for them, and re-layouts  9.61 us (12%)
    pallas_call x1, Pallas kernels, per_device(): pl.pallas_call(functools.partial(kernel, (frames, dps, chunks, chunk, win...  70.9 us
    unnamed x17, local copies, waits for them, and re-layouts  9.61 us

profile of v1, /device:TPU:1, one launch (start us, length us, event | category | flops | bytes accessed | tf_op | source)
XLA Modules:
  0.0 81.2 jit_solution(13904274767705766775)
XLA Ops:
  0.6 0.9 %copy.10.blocks_hbm = s32[32,3,4,4]{3,2,1,0:T(4,128)S(1)} copy(s32[32,3,4,4]{0,3,2,1:T(4,128)} %param.13) | data formatting | bytes 12288 | tf_op args[5]
  1.5 0.0 copy-start
  1.5 1.3 %copy-done = bf16[1,128,5120]{2,1,0:T(8,128)(2,1)S(1)} copy-done((bf16[1,128,5120]{2,1,0:T(8,128)(2,1)S(1)}, bf16[1,128,5120]{2,1,0:T(8,128)(2,1)}, u32[]{:S(2)}) %copy-start) | copy-done | bytes 1310744
  2.9 0.0 copy-start.1
  2.9 1.1 %copy-done.1 = bf16[1,128,2560]{2,1,0:T(8,128)(2,1)S(1)} copy-done((bf16[1,128,2560]{2,1,0:T(8,128)(2,1)S(1)}, bf16[1,128,2560]{2,1,0:T(8,128)(2,1)}, u32[]{:S(2)}) %copy-start.1) | copy-done | bytes 655384
  3.9 0.0 copy-start.2
  3.9 1.1 %copy-done.2 = bf16[1,128,2560]{2,1,0:T(8,128)(2,1)S(1)} copy-done((bf16[1,128,2560]{2,1,0:T(8,128)(2,1)S(1)}, bf16[1,128,2560]{2,1,0:T(8,128)(2,1)}, u32[]{:S(2)}) %copy-start.2) | copy-done | bytes 655384
  5.0 0.0 copy-start.3
  5.0 1.1 %copy-done.3 = bf16[1,128,2560]{2,1,0:T(8,128)(2,1)S(1)} copy-done((bf16[1,128,2560]{2,1,0:T(8,128)(2,1)S(1)}, bf16[1,128,2560]{2,1,0:T(8,128)(2,1)}, u32[]{:S(2)}) %copy-start.3) | copy-done | bytes 655384
  6.1 0.0 copy-start.4
  6.1 1.1 %copy-done.4 = bf16[1,128,2560]{2,1,0:T(8,128)(2,1)S(1)} copy-done((bf16[1,128,2560]{2,1,0:T(8,128)(2,1)S(1)}, bf16[1,128,2560]{2,1,0:T(8,128)(2,1)}, u32[]{:S(2)}) %copy-start.4) | copy-done | bytes 655384
  7.2 0.0 copy-start.5
  7.2 0.9 %copy-done.5 = bf16[3,8,5120]{2,1,0:T(8,128)(2,1)S(1)} copy-done((bf16[3,8,5120]{2,1,0:T(8,128)(2,1)S(1)}, bf16[3,8,5120]{2,1,0:T(8,128)(2,1)}, u32[]{:S(2)}) %copy-start.5) | copy-done | bytes 245784
  8.1 0.0 copy-start.6
  8.1 0.9 %copy-done.6 = bf16[3,8,2560]{2,1,0:T(8,128)(2,1)S(1)} copy-done((bf16[3,8,2560]{2,1,0:T(8,128)(2,1)S(1)}, bf16[3,8,2560]{2,1,0:T(8,128)(2,1)}, u32[]{:S(2)}) %copy-start.6) | copy-done | bytes 122904
  9.0 70.9 %shard_map.95 = (f32[3,8,160]{2,1,0:T(8,128)S(1)}, f32[3,8,80]{2,1,0:T(8,128)S(1)}) custom-call(bf16[1,128,2560]{2,1,0:T(8,128)(2,1)S(1)} %copy-done.1, bf16[1,128,2560]{2,1,0:T(8,128)(2,1)S(1)} %copy-done.2, bf16[1,128,2560]{2,1,0:T(8,128)(2,1)S(1)} %copy-done.3, bf16[1,128,2560]{2,1,0:T(8,128)(2,1)S(1)} %copy-done.4, bf16[1,128,5120]{2,1,0:T(8,128)(2,1)S(1)} %copy-done, ...), custom_call_target="tpu_custom_call" | custom-call | tf_op jit(solution)/shard_map/pallas_call | solution.py:278
  80.0 0.6 copy.13
  80.6 0.6 copy.14
Async XLA Ops:
  1.5 1.3 %copy-start = (bf16[1,128,5120]{2,1,0:T(8,128)(2,1)S(1)}, bf16[1,128,5120]{2,1,0:T(8,128)(2,1)}, u32[]{:S(2)}) copy-start(bf16[1,128,5120]{2,1,0:T(8,128)(2,1)} %x_hbm.1) | copy-start | bytes 3932164
  2.9 1.1 %copy-start.1 = (bf16[1,128,2560]{2,1,0:T(8,128)(2,1)S(1)}, bf16[1,128,2560]{2,1,0:T(8,128)(2,1)}, u32[]{:S(2)}) copy-start(bf16[1,128,2560]{2,1,0:T(8,128)(2,1)} %q_hbm.1) | copy-start | bytes 1966084
  3.9 1.1 %copy-start.2 = (bf16[1,128,2560]{2,1,0:T(8,128)(2,1)S(1)}, bf16[1,128,2560]{2,1,0:T(8,128)(2,1)}, u32[]{:S(2)}) copy-start(bf16[1,128,2560]{2,1,0:T(8,128)(2,1)} %k_hbm.1) | copy-start | bytes 1966084
  5.0 1.1 %copy-start.3 = (bf16[1,128,2560]{2,1,0:T(8,128)(2,1)S(1)}, bf16[1,128,2560]{2,1,0:T(8,128)(2,1)}, u32[]{:S(2)}) copy-start(bf16[1,128,2560]{2,1,0:T(8,128)(2,1)} %v_hbm.1) | copy-start | bytes 1966084
  6.1 1.1 %copy-start.4 = (bf16[1,128,2560]{2,1,0:T(8,128)(2,1)S(1)}, bf16[1,128,2560]{2,1,0:T(8,128)(2,1)}, u32[]{:S(2)}) copy-start(bf16[1,128,2560]{2,1,0:T(8,128)(2,1)} %g_hbm.1) | copy-start | bytes 1966084
  7.2 0.9 %copy-start.5 = (bf16[3,8,5120]{2,1,0:T(8,128)(2,1)S(1)}, bf16[3,8,5120]{2,1,0:T(8,128)(2,1)}, u32[]{:S(2)}) copy-start(bf16[3,8,5120]{2,1,0:T(8,128)(2,1)} %a_hbm.1) | copy-start | bytes 737284
  8.1 0.9 %copy-start.6 = (bf16[3,8,2560]{2,1,0:T(8,128)(2,1)S(1)}, bf16[3,8,2560]{2,1,0:T(8,128)(2,1)}, u32[]{:S(2)}) copy-start(bf16[3,8,2560]{2,1,0:T(8,128)(2,1)} %u_hbm.1) | copy-start | bytes 368644

commit v2 on v1

--- a/solution.py
+++ b/solution.py
@@ -49,8 +49,8 @@
     local = [
         pltpu.make_async_copy(src, dst, local_sem.at[i])
         for i, (src, dst) in enumerate([
-            (q_hbm.at[0], qb), (k_hbm.at[0], kb.at[1]), (v_hbm.at[0], vb.at[1]), (g_hbm.at[0], gb),
-            (x_hbm.at[0], xb), (a_hbm, ab), (u_hbm, ub), (blocks_hbm.at[frame], bb),
+            (k_hbm.at[0], kb.at[1]), (v_hbm.at[0], vb.at[1]), (q_hbm.at[0], qb), (g_hbm.at[0], gb),
+            (x_hbm.at[0], xb), (a_hbm, ab), (u_hbm, ub), (blocks_hbm, bb),
         ])
     ]
     for copy in local:
@@ -67,8 +67,8 @@
 
     def halo_copy(c, side, kind):
         cols = pl.ds(pl.multiple_of(c * chunk, 128), chunk)
-        src, dst = ((k_hbm, kb), (v_hbm, vb))[kind]
-        return remote(src.at[0, :, cols], dst.at[2 * side, :, cols],
+        both = (kb, vb)[kind]
+        return remote(both.at[1, :, cols], both.at[2 * side, :, cols],
                       ks_sem.at[side, kind, c], kr_sem.at[side, kind, c], halo[side])
 
     def halo_start(c):
@@ -76,20 +76,24 @@
             for side in range(2):
                 halo_copy(c, side, kind).start()
 
+    for i in range(2):
+        local[i].wait()
+
     @pl.loop(0, window)
     def _(c):
         halo_start(c)
 
     local[7].wait()
-    lane_block = lax.broadcasted_iota(jnp.int32, (1, tokens), 1) // (tokens // 4)
+    lane_block = lax.broadcasted_iota(jnp.int32, (4, tokens), 1) // (tokens // 4)
+    mine = lax.broadcasted_iota(jnp.int32, (4, frames), 1) == frame
     for o in range(3):
-        table = bb[o]
+        lines = jnp.zeros((4, tokens), jnp.int32)
+        for a in range(4):
+            kept = jnp.sum(jnp.where(mine, bb[o, a], 0), axis=1, keepdims=True)
+            lines = jnp.where(lane_block == a, jnp.broadcast_to(kept, (4, tokens)), lines)
+        lines = jnp.where(lines > 0, 0.0, MASKED).astype(F32)
         for b in range(4):
-            row = jnp.zeros((1, tokens), jnp.int32)
-            for a in range(4):
-                row = jnp.where(lane_block == a, jnp.broadcast_to(table[a:a + 1, b:b + 1], (1, tokens)), row)
-            line = jnp.where(row > 0, 0.0, MASKED).astype(F32)
-            bias[pl.ds(o * tokens + b * (tokens // 4), tokens // 4), :] = jnp.broadcast_to(line, (tokens // 4, tokens))
+            bias[pl.ds(o * tokens + b * (tokens // 4), tokens // 4), :] = jnp.broadcast_to(lines[b:b + 1], (tokens // 4, tokens))
 
     local[6].wait()
     uall[...] = jnp.concatenate([ub[1].astype(F32), ub[2].astype(F32), ub[0].astype(F32), ub[0].astype(F32)], 0).astype(BF16)
@@ -105,7 +109,7 @@
     midq[...] = jnp.zeros_like(midq)
     midkv[...] = jnp.zeros_like(midkv)
     upb[...] = jnp.zeros_like(upb)
-    for i in range(4):
+    for i in range(2, 4):
         local[i].wait()
 
     def up_step(p):
@@ -262,7 +266,7 @@
         vmem((tokens, width), BF16), vmem((tokens, width), BF16),
         vmem((3, tokens, width), BF16), vmem((3, tokens, width), BF16),
         vmem((tokens, model), BF16), vmem((3, RANK, model), BF16), vmem((3, RANK, width), BF16),
-        vmem((3, 4, 4), jnp.int32), vmem((3 * tokens, tokens), F32),
+        vmem((3, 4, 4, frames), jnp.int32), vmem((3 * tokens, tokens), F32),
         vmem((3, 2 * RANK, tokens), BF16), vmem((2 * RANK, tokens), BF16), vmem((4 * RANK, width), BF16),
         vmem((tokens, width), BF16), vmem((3 * tokens, width), BF16), vmem((3 * tokens, width), BF16),
         vmem((RANK, tokens), F32), vmem((3, 2 * RANK, tokens), F32), vmem((2, 2 * RANK, tokens), F32),
@@ -284,8 +288,8 @@
         in_specs=[pl.BlockSpec(memory_space=pltpu.HBM)] * 8,
         out_specs=(pl.BlockSpec(memory_space=pltpu.VMEM), pl.BlockSpec(memory_space=pltpu.VMEM)),
         scratch_shapes=scratch,
-        compiler_params=pltpu.CompilerParams(collective_id=0, has_side_effects=True, vmem_limit_bytes=48 << 20),
-    )(q, k, v, g, x, blocks, a, u)
+        compiler_params=pltpu.CompilerParams(collective_id=0, has_side_effects=True, vmem_limit_bytes=60 << 20),
+    )(q, k, v, g, x, jnp.transpose(blocks, (1, 2, 3, 0)), a, u)
 
 
 def solution(mesh):

time: 81.6 us -> 73.7 us (0.903)
  local copies, waits for them, and re-layouts: 9.61 us -> 2.65 us
    unnamed x17 -> x2, local copies, waits for them, and re-layouts: 9.61 us -> 2.65 us
where the time goes in v2:
time: 73.7 us; the launch traced here: 73.4 us
  Pallas kernels  70.1 us (95%)
  local copies, waits for them, and re-layouts  2.65 us (4%)
    pallas_call x1, Pallas kernels, per_device(): pl.pallas_call(functools.partial(kernel, (frames, dps, chunks, chunk, win...  70.1 us
    unnamed x2, local copies, waits for them, and re-layouts  2.65 us

profile of v2, /device:TPU:1, one launch (start us, length us, event | category | flops | bytes accessed | tf_op | source)
XLA Modules:
  0.0 73.4 jit_solution(7688139860838363280)
XLA Ops:
  0.6 70.1 %shard_map.95 = (f32[3,8,160]{2,1,0:T(8,128)}, f32[3,8,80]{2,1,0:T(8,128)}) custom-call(bf16[1,128,2560]{2,1,0:T(8,128)(2,1)} %q_hbm.1, bf16[1,128,2560]{2,1,0:T(8,128)(2,1)} %k_hbm.1, bf16[1,128,2560]{2,1,0:T(8,128)(2,1)} %v_hbm.1, bf16[1,128,2560]{2,1,0:T(8,128)(2,1)} %g_hbm.1, bf16[1,128,5120]{2,1,0:T(8,128)(2,1)} %x_hbm.1, s32[3,4,4,32]{3,2,1,0:T(4,128)} %bitcast.1, ...), custom_call_target="tpu_custom_call" | custom-call | tf_op jit(solution)/shard_map/pallas_call | solution.py:282
  70.8 1.3 %copy.12 = f32[3,8,160]{2,1,0:T(8,128)} copy(f32[3,8,160]{2,1,0:T(8,128)} %get-tuple-element.4) | data formatting | bytes 30720
  72.1 1.3 %copy.13 = f32[3,8,80]{2,1,0:T(8,128)} copy(f32[3,8,80]{2,1,0:T(8,128)} %get-tuple-element.5) | data formatting | bytes 15360

commit v3 on v2

v3 whole, which is shorter than its diff:
```python
import functools
import math

import jax
import jax.numpy as jnp
from jax import lax
from jax.experimental import pallas as pl
from jax.experimental.pallas import tpu as pltpu
from jax.sharding import PartitionSpec as P

HEAD = 128
RANK = 8
ADAPTER_SCALE = 2.0
MASKED = -1e30
CHIPS_X = 4
MESH = pl.DeviceIdType.MESH
BF16 = jnp.bfloat16
F32 = jnp.float32
NT = (((1,), (1,)), ((), ()))
NN = (((1,), (0,)), ((), ()))
TN = (((0,), (0,)), ((), ()))


def dot(a, b, dims=NN):
    return lax.dot_general(a, b, dims, preferred_element_type=F32)


def far_first(n):
    return sorted(range(n - 1), key=lambda i: -min(i + 1, n - 1 - i))


def kernel(cfg, q_hbm, k_hbm, v_hbm, g_hbm, x_hbm, blocks_hbm, a_hbm, u_hbm, down_out, up_out, *scratch):
    (qb, gb, kb, vb, xb, ab, ub, bb, bias, lowb, lowq, uall, gqb, gkb, gvb, midkv, mrx, msib, db, upb, ups, upr, st,
     xsb, xrx, zb, zf, zrx, ysb, yrx, fb,
     local_sem, ks_sem, kr_sem, ls_sem, lr_sem, ms_sem, mr_sem, us_sem, ur_sem, is_sem, ir_sem, xs_sem, xr_sem, zs_sem, zr_sem,
     ys_sem, yr_sem, fs_sem, fr_sem) = scratch
    frames, dps, chunks, chunk, window, up_width, lag = cfg
    X, Y = CHIPS_X, dps // 2
    Z = frames // X
    width, model = qb.shape[1], xb.shape[2]
    tokens = qb.shape[0]
    span = 3 * tokens
    dp = lax.axis_index("dp")
    frame = lax.axis_index("frames")
    y, core = dp // 2, dp % 2
    z, x = frame // X, frame % X
    other = y * 2 + 1 - core
    sibling = (other, frame)
    halo = [(dp, (frame + 1) % frames), (dp, (frame + frames - 1) % frames)]
    halo_other = [(other, (frame + 1) % frames), (other, (frame + frames - 1) % frames)]
    xs = [(dp, z * X + (x + d) % X) for d in range(1, X)]
    zs = [(dp, ((z + d) % Z) * X + x) for d in range(1, Z)]
    ys = [(((y + d) % Y) * 2 + core, frame) for d in range(1, Y)]

    has_next, has_prev = frame < frames - 1, frame > 0
    can_send, can_recv = (has_next, has_prev), (has_prev, has_next)
    barrier = pltpu.get_barrier_semaphore()

    def greet(peer):
        pl.semaphore_signal(barrier, inc=1, device_id=peer, device_id_type=MESH)

    for side in range(2):
        @pl.when(can_send[side])
        def _():
            greet(halo[side])
            greet(halo_other[side])
    others = [sibling] + xs + zs + ys
    for peer in others:
        greet(peer)
    local = [
        pltpu.make_async_copy(src, dst, local_sem.at[i])
        for i, (src, dst) in enumerate([
            (k_hbm.at[0], kb.at[1]), (v_hbm.at[0], vb.at[1]), (q_hbm.at[0], qb), (g_hbm.at[0], gb),
            (x_hbm.at[0], xb.at[0]), (a_hbm, ab), (u_hbm, ub), (blocks_hbm, bb),
        ])
    ]
    for copy in local:
        copy.start()
    for side, (slot, absent) in enumerate(((0, frame == 0), (2, frame == frames - 1))):
        @pl.when(absent)
        def _():
            kb[slot] = jnp.zeros((tokens, width), BF16)
            vb[slot] = jnp.zeros((tokens, width), BF16)
            lowb[slot] = jnp.zeros((2 * RANK, tokens), BF16)
            for video in range(2):
                mrx[video, side] = jnp.zeros((2 * RANK, tokens), F32)
    pl.semaphore_wait(barrier, len(others) + 2 * (has_next.astype(jnp.int32) + has_prev.astype(jnp.int32)))

    def remote(src, dst, send, recv, peer):
        return pltpu.make_async_remote_copy(
            src_ref=src, dst_ref=dst, send_sem=send, recv_sem=recv, device_id=peer, device_id_type=MESH)

    def halo_copy(c, side, kind):
        cols = pl.ds(pl.multiple_of(c * chunk, 128), chunk)
        both = (kb, vb)[kind]
        return remote(both.at[1, :, cols], both.at[2 * side, :, cols],
                      ks_sem.at[side, kind, c], kr_sem.at[side, kind, c], halo[side])

    def halo_start(c):
        for side in range(2):
            @pl.when(can_send[side])
            def _():
                for kind in range(2):
                    halo_copy(c, side, kind).start()

    for i in range(2):
        local[i].wait()

    @pl.loop(0, window)
    def _(c):
        halo_start(c)

    local[7].wait()
    lane_block = lax.broadcasted_iota(jnp.int32, (4, tokens), 1) // (tokens // 4)
    mine = lax.broadcasted_iota(jnp.int32, (4, frames), 1) == frame
    for o in range(3):
        lines = jnp.zeros((4, tokens), jnp.int32)
        for a in range(4):
            kept = jnp.sum(jnp.where(mine, bb[o, a], 0), axis=1, keepdims=True)
            lines = jnp.where(lane_block == a, jnp.broadcast_to(kept, (4, tokens)), lines)
        lines = jnp.where(lines > 0, 0.0, MASKED).astype(F32)
        for b in range(4):
            bias[pl.ds(o * tokens + b * (tokens // 4), tokens // 4), :] = jnp.broadcast_to(lines[b:b + 1], (tokens // 4, tokens))

    local[6].wait()
    uall[...] = jnp.concatenate([ub[1].astype(F32), ub[2].astype(F32), ub[0].astype(F32), ub[0].astype(F32)], 0).astype(BF16)
    local[5].wait()
    local[4].wait()
    input_copy = remote(xb.at[0], xb.at[1], is_sem, ir_sem, sibling)
    input_copy.start()
    stacked = jnp.concatenate([ab[1].astype(F32), ab[2].astype(F32), ab[0].astype(F32), ab[0].astype(F32)], 0).astype(BF16)
    low = dot(stacked, xb[0], NT).astype(BF16)
    lowb[1] = low[0:2 * RANK]
    lowq[...] = low[2 * RANK:4 * RANK]
    low_copies = [remote(lowb.at[1], lowb.at[2 * side], ls_sem.at[side], lr_sem.at[side], halo[side]) for side in range(2)]
    for side in range(2):
        pl.when(can_send[side])(low_copies[side].start)
    midkv[...] = jnp.zeros_like(midkv)
    upb[...] = jnp.zeros_like(upb)
    for i in range(2, 4):
        local[i].wait()

    def up_copy(p):
        cols = pl.ds(pl.multiple_of(p * up_width, 128), up_width)
        return remote(ups.at[:, cols], upr.at[:, cols], us_sem.at[p], ur_sem.at[p], sibling)

    def up_step(p):
        cols = pl.ds(pl.multiple_of(p * up_width, 128), up_width)
        lows = jnp.concatenate([lowb[0], lowb[1], lowb[2]], 1)
        up_k = dot(lows, gkb[:, cols])[0:RANK]
        up_v = dot(lows, gvb[:, cols])[RANK:2 * RANK]
        up_q = dot(lowq[...], gqb[:, cols])[0:RANK]
        both = ADAPTER_SCALE * jnp.concatenate([up_k, up_v, up_q], 0)
        upb[:, cols] = both
        ups[:, cols] = jnp.concatenate([both, up_q], 0).astype(BF16)
        up_copy(p).start()

    scale = HEAD ** -0.5
    scale2 = scale * math.log2(math.e)
    steps_inside = len([c for c in range(lag, chunks) if (c - lag + 1) * up_width <= c * chunk])

    @pl.loop(0, chunks)
    def _(c):
        for side in range(2):
            @pl.when(can_send[side])
            def _():
                for kind in range(2):
                    halo_copy(c, side, kind).wait_send()

            @pl.when(can_recv[side])
            def _():
                for kind in range(2):
                    halo_copy(c, side, kind).wait_recv()

        @pl.when(c + window < chunks)
        def _():
            halo_start(c + window)

        @pl.when(c == lag)
        def _():
            for side in range(2):
                pl.when(can_send[side])(low_copies[side].wait_send)
                pl.when(can_recv[side])(low_copies[side].wait_recv)

        @pl.when((c >= lag) & (c < lag + steps_inside))
        def _():
            up_step(c - lag)

        for h in range(chunk // HEAD):
            cols = pl.ds(pl.multiple_of(c * chunk + h * HEAD, 128), HEAD)
            q, g = qb[:, cols], gb[:, cols]
            kc = kb[:, :, cols].reshape(span, HEAD)
            vc = vb[:, :, cols].reshape(span, HEAD)
            s = dot(kc, q, NT) * scale2 + bias[...]
            e = jnp.exp2(s - jnp.max(s, axis=0, keepdims=True))
            w = e * (1.0 / jnp.sum(e, axis=0, keepdims=True))
            wg = dot(vc, g, NT)
            delta = jnp.sum(w * wg, axis=0, keepdims=True)
            ds = (w * (wg - delta)).astype(BF16)
            gkb[:, cols] = (dot(ds, q) * scale).astype(BF16)
            gvb[:, cols] = dot(w.astype(BF16), g).astype(BF16)
            gqb[:, cols] = (dot(ds, kc, TN) * scale).astype(BF16)
        cols = pl.ds(pl.multiple_of(c * chunk, 128), chunk)
        ukv, uq = uall[0:2 * RANK, cols], uall[2 * RANK:4 * RANK, cols]
        mk = dot(ukv, gkb[:, cols], NT)
        mv = dot(ukv, gvb[:, cols], NT)
        midkv[1, 2 * RANK:3 * RANK] += dot(uq, gqb[:, cols], NT)[0:RANK]
        for o in range(3):
            part = slice(o * tokens, (o + 1) * tokens)
            midkv[o, 0:2 * RANK] += jnp.concatenate([mk[0:RANK, part], mv[RANK:2 * RANK, part]], 0)

    mid_copies = []
    for video, peers in enumerate((halo, halo_other)):
        for side in range(2):
            mid_copies.append(remote(midkv.at[2 - 2 * side, pl.ds(0, 2 * RANK)], mrx.at[video, side],
                                     ms_sem.at[video, side], mr_sem.at[video, side], peers[side]))
    own_copy = remote(midkv.at[1], msib, ms_sem.at[2, 0], mr_sem.at[2, 0], sibling)
    for i in (2, 0, 3, 1):
        pl.when(can_send[i % 2])(mid_copies[i].start)
    own_copy.start()
    for p in range(steps_inside, width // up_width):
        up_step(p)
    input_copy.wait_recv()
    own_copy.wait_recv()
    for i in range(4):
        pl.when(can_recv[i % 2])(mid_copies[i].wait_recv)
    mids = []
    for video, own in enumerate((midkv, msib)):
        own = own[1] if video == 0 else own[...]
        terms = mrx[video, 0] + mrx[video, 1]
        mids.append((ADAPTER_SCALE * jnp.concatenate([own[0:2 * RANK] + terms, own[2 * RANK:3 * RANK]], 0)).astype(BF16))
    db[...] = dot(jnp.concatenate(mids, 1), xb[...].reshape(2 * tokens, model))
    for p in range(width // up_width):
        up_copy(p).wait_recv()

    down_block, up_block = model // frames, width // frames
    rows = 3 * RANK
    lane = lax.broadcasted_iota(jnp.int32, (rows, 128), 1)

    def blocks_of(to):
        wide = [db[:, pl.ds(pl.multiple_of(zz * X * down_block + to * 128, 128), 256)] for zz in range(Z)]
        turned = [pltpu.roll(w, lax.rem(256 - 32 * to, 256), 1) for w in wide]
        return turned

    @pl.when(core == 1)
    def _():
        upb[:, 0:width] += upr[0:rows].astype(F32)

    def left_half(to):
        return jnp.concatenate([t[:, 0:128] for t in blocks_of(to)], 0)

    def right_half(to):
        out = []
        for zz, turned in enumerate(blocks_of(to)):
            start = zz * X * up_block + to * up_block
            tile = pl.multiple_of(start // 128 * 128, 128)
            third = upb[:, pl.ds(tile, 256)]
            third = pltpu.roll(third, lax.rem(256 + 32 - start % 128, 256), 1)[:, 0:128]
            out.append(jnp.where(lane < 32, turned[:, 128:256], jnp.where(lane < 32 + up_block, third, 0.0)))
        return jnp.concatenate(out, 0)

    x_copies = [remote(xsb.at[i], xrx.at[i], xs_sem.at[i], xr_sem.at[i], xs[i]) for i in range(X - 1)]

    def send_half(half):
        for i in (1, 0, 2):
            xsb[i] = half((x + 1 + i) % X).astype(BF16)
            x_copies[i].start()
        st[...] = half(x)

    @pl.when(core == 0)
    def _():
        send_half(left_half)

    @pl.when(core == 1)
    def _():
        send_half(right_half)

    total = st[...]
    for i in range(X - 1):
        x_copies[i].wait_recv()
        total = total + xrx[i].astype(F32)
    total = total.reshape(Z, rows, 128)
    zf[...] = total
    zb[...] = jnp.concatenate([total, jnp.zeros((Z, 32 - rows, 128), F32)], 1).astype(BF16)
    z_copies = [remote(zb.at[(z + 1 + i) % Z], zrx.at[i], zs_sem.at[i], zr_sem.at[i], zs[i]) for i in range(Z - 1)]
    for i in far_first(Z):
        z_copies[i].start()
    total = zf[z]
    for i in range(Z - 1):
        z_copies[i].wait_recv()
        total = total + zrx[i].astype(F32)[0:rows]
    mine = jnp.concatenate([total, jnp.zeros((32 - rows, 128), F32)], 0).astype(BF16)
    ysb[...] = mine
    y_copies = [remote(ysb, yrx.at[y], ys_sem.at[i], yr_sem.at[i], ys[i]) for i in range(Y - 1)]
    for i in far_first(Y):
        y_copies[i].start()
    yrx[y] = mine
    for copy in y_copies:
        copy.wait_recv()
    total = yrx[0].astype(F32)
    for i in range(1, Y):
        total = total + yrx[i].astype(F32)
    fb[core] = total[0:rows]
    last = remote(fb.at[core], fb.at[core], fs_sem, fr_sem, sibling)
    last.start()
    last.wait_recv()
    left, right = fb[0], fb[1]
    shifted = pltpu.roll(right, 128 - 32, 1)
    for place, c in enumerate((1, 2, 0)):
        part = slice(place * RANK, (place + 1) * RANK)
        down_out[c, :, 0:128] = left[part]
        down_out[c, :, 128:down_block] = right[part, 0:down_block - 128]
        up_out[c] = shifted[part, 0:up_block]
    for p in range(width // up_width):
        up_copy(p).wait_send()
    for i in range(4):
        pl.when(can_send[i % 2])(mid_copies[i].wait_send)
    for copy in [input_copy, own_copy] + x_copies + z_copies + y_copies + [last]:
        copy.wait_send()


def per_device(frames, dps, q, k, v, g, x, blocks, a, u):
    tokens, width = q.shape[1:]
    model = x.shape[2]
    heads = width // HEAD
    chunk = 2 * HEAD if heads % 4 == 0 else HEAD
    chunks = width // chunk
    window = min(4, chunks)
    up_width = 2 * chunk if heads % 4 == 0 else chunk
    lag = chunks // 2 if heads % 4 == 0 else 3
    Y, Z, X = dps // 2, frames // CHIPS_X, CHIPS_X
    rows = 3 * RANK
    vmem = pltpu.VMEM
    dma = pltpu.SemaphoreType.DMA
    scratch = [
        vmem((tokens, width), BF16), vmem((tokens, width), BF16),
        vmem((3, tokens, width), BF16), vmem((3, tokens, width), BF16),
        vmem((2, tokens, model), BF16), vmem((3, RANK, model), BF16), vmem((3, RANK, width), BF16),
        vmem((3, 4, 4, frames), jnp.int32), vmem((3 * tokens, tokens), F32),
        vmem((3, 2 * RANK, tokens), BF16), vmem((2 * RANK, tokens), BF16), vmem((4 * RANK, width), BF16),
        vmem((tokens, width), BF16), vmem((3 * tokens, width), BF16), vmem((3 * tokens, width), BF16),
        vmem((3, rows, tokens), F32), vmem((2, 2, 2 * RANK, tokens), F32), vmem((rows, tokens), F32),
        vmem((rows, model), F32), vmem((rows, width + 128), F32), vmem((4 * RANK, width), BF16), vmem((4 * RANK, width), BF16),
        vmem((Z * rows, 128), F32),
        vmem((X - 1, Z * rows, 128), BF16), vmem((X - 1, Z * rows, 128), BF16),
        vmem((Z, 32, 128), BF16), vmem((Z, rows, 128), F32), vmem((max(Z - 1, 1), 32, 128), BF16),
        vmem((32, 128), BF16), vmem((Y, 32, 128), BF16), vmem((2, rows, 128), F32),
        dma((8,)), dma((2, 2, chunks)), dma((2, 2, chunks)), dma((2,)), dma((2,)), dma((3, 2)), dma((3, 2)),
        dma((width // up_width,)), dma((width // up_width,)), dma, dma, dma((X - 1,)), dma((X - 1,)), dma((max(Z - 1, 1),)), dma((max(Z - 1, 1),)),
        dma((max(Y - 1, 1),)), dma((max(Y - 1, 1),)), dma, dma,
    ]
    return pl.pallas_call(
        functools.partial(kernel, (frames, dps, chunks, chunk, window, up_width, lag)),
        out_shape=(
            jax.ShapeDtypeStruct((3, RANK, model // frames), F32),
            jax.ShapeDtypeStruct((3, RANK, width // frames), F32),
        ),
        in_specs=[pl.BlockSpec(memory_space=pltpu.HBM)] * 8,
        out_specs=(pl.BlockSpec(memory_space=pltpu.VMEM), pl.BlockSpec(memory_space=pltpu.VMEM)),
        scratch_shapes=scratch,
        compiler_params=pltpu.CompilerParams(collective_id=0, has_side_effects=True, vmem_limit_bytes=60 << 20),
    )(q, k, v, g, x, jnp.transpose(blocks, (1, 2, 3, 0)), a, u)


def solution(mesh):
    split = P("dp", "frames", None)
    return jax.shard_map(
        functools.partial(per_device, mesh.shape["frames"], mesh.shape["dp"]),
        mesh=mesh,
        in_specs=(split,) * 5 + (P(), P(), P()),
        out_specs=(P(None, None, "frames"), P(None, None, "frames")),
        check_vma=False,
    )
```

time: 73.7 us -> 72.7 us (0.986)
  Pallas kernels: 70.1 us -> 69.1 us
    pallas_call x1, Pallas kernels: 70.1 us -> 69.1 us  [per_device(): pl.pallas_call(functools.partial(kernel, (frames, dps, chunks, chunk, win...]
where the time goes in v3:
time: 72.7 us; the launch traced here: 72.4 us
  Pallas kernels  69.1 us (95%)
  local copies, waits for them, and re-layouts  2.65 us (4%)
    pallas_call x1, Pallas kernels, per_device(): pl.pallas_call(functools.partial(kernel, (frames, dps, chunks, chunk, win...  69.1 us
    unnamed x2, local copies, waits for them, and re-layouts  2.65 us

profile of v3, /device:TPU:1, one launch (start us, length us, event | category | flops | bytes accessed | tf_op | source)
XLA Modules:
  0.0 72.4 jit_solution(13306016396245805343)
XLA Ops:
  0.6 69.1 %shard_map.95 = (f32[3,8,160]{2,1,0:T(8,128)}, f32[3,8,80]{2,1,0:T(8,128)}) custom-call(bf16[1,128,2560]{2,1,0:T(8,128)(2,1)} %q_hbm.1, bf16[1,128,2560]{2,1,0:T(8,128)(2,1)} %k_hbm.1, bf16[1,128,2560]{2,1,0:T(8,128)(2,1)} %v_hbm.1, bf16[1,128,2560]{2,1,0:T(8,128)(2,1)} %g_hbm.1, bf16[1,128,5120]{2,1,0:T(8,128)(2,1)} %x_hbm.1, s32[3,4,4,32]{3,2,1,0:T(4,128)} %bitcast.1, ...), custom_call_target="tpu_custom_call" | custom-call | tf_op jit(solution)/shard_map/pallas_call | solution.py:352
  69.8 1.3 %copy.12 = f32[3,8,160]{2,1,0:T(8,128)} copy(f32[3,8,160]{2,1,0:T(8,128)} %get-tuple-element.4) | data formatting | bytes 30720
  71.1 1.3 %copy.13 = f32[3,8,80]{2,1,0:T(8,128)} copy(f32[3,8,80]{2,1,0:T(8,128)} %get-tuple-element.5) | data formatting | bytes 15360

commit v4 on v3

--- a/solution.py
+++ b/solution.py
@@ -29,8 +29,8 @@
     return sorted(range(n - 1), key=lambda i: -min(i + 1, n - 1 - i))
 
 
-def kernel(cfg, q_hbm, k_hbm, v_hbm, g_hbm, x_hbm, blocks_hbm, a_hbm, u_hbm, down_out, up_out, *scratch):
-    (qb, gb, kb, vb, xb, ab, ub, bb, bias, lowb, lowq, uall, gqb, gkb, gvb, midkv, mrx, msib, db, upb, ups, upr, st,
+def kernel(cfg, q_hbm, k_hbm, v_hbm, g_hbm, x_hbm, blocks_hbm, a_hbm, u_hbm, out, *scratch):
+    (qb, gb, kb, vb, xb, ab, ub, bb, bias, lowb, lowq, uall, gqb, gkb, gvb, midkv, mrx, msib, xp, upl, upb, ups, upr, st,
      xsb, xrx, zb, zf, zrx, ysb, yrx, fb,
      local_sem, ks_sem, kr_sem, ls_sem, lr_sem, ms_sem, mr_sem, us_sem, ur_sem, is_sem, ir_sem, xs_sem, xr_sem, zs_sem, zr_sem,
      ys_sem, yr_sem, fs_sem, fr_sem) = scratch
@@ -140,6 +140,20 @@
     for i in range(2, 4):
         local[i].wait()
 
+    down_block, up_block = model // frames, width // frames
+    rows = 3 * RANK
+    lane = lax.broadcasted_iota(jnp.int32, (rows, 128), 1)
+    upl[...] = jnp.zeros_like(upl)
+
+    def lay_out(to):
+        keep = lax.broadcasted_iota(jnp.int32, (2 * tokens, 128), 1) < 32
+        for zz in range(Z):
+            start = (zz * X + to) * down_block
+            wide = xb[:, :, start // 128 * 128:start // 128 * 128 + 256].reshape(2 * tokens, 256).astype(F32)
+            wide = pltpu.roll(wide, (256 - start % 128) % 256, 1)
+            right = jnp.where(keep, wide[:, 128:256], 0.0)
+            xp[to, :, zz * 128:(zz + 1) * 128] = jnp.where(core == 0, wide[:, 0:128], right).astype(BF16)
+
     def up_copy(p):
         cols = pl.ds(pl.multiple_of(p * up_width, 128), up_width)
         return remote(ups.at[:, cols], upr.at[:, cols], us_sem.at[p], ur_sem.at[p], sibling)
@@ -181,6 +195,13 @@
             for side in range(2):
                 pl.when(can_send[side])(low_copies[side].wait_send)
                 pl.when(can_recv[side])(low_copies[side].wait_recv)
+
+        for to in range(X):
+            @pl.when(c == chunks - X - 1 + to)
+            def _():
+                if to == 0:
+                    input_copy.wait_recv()
+                lay_out(to)
 
         @pl.when((c >= lag) & (c < lag + steps_inside))
         def _():
@@ -220,7 +241,19 @@
     own_copy.start()
     for p in range(steps_inside, width // up_width):
         up_step(p)
-    input_copy.wait_recv()
+    for p in range(width // up_width):
+        up_copy(p).wait_recv()
+
+    @pl.when(core == 1)
+    def _():
+        upb[:, 0:width] += upr[0:rows].astype(F32)
+        for to in range(X):
+            for zz in range(Z):
+                start = (zz * X + to) * up_block
+                third = upb[:, start // 128 * 128:start // 128 * 128 + 256]
+                third = pltpu.roll(third, (256 + 32 - start % 128) % 256, 1)[:, 0:128]
+                upl[to, zz * rows:(zz + 1) * rows] = jnp.where((lane >= 32) & (lane < 32 + up_block), third, 0.0)
+
     own_copy.wait_recv()
     for i in range(4):
         pl.when(can_recv[i % 2])(mid_copies[i].wait_recv)
@@ -229,52 +262,18 @@
         own = own[1] if video == 0 else own[...]
         terms = mrx[video, 0] + mrx[video, 1]
         mids.append((ADAPTER_SCALE * jnp.concatenate([own[0:2 * RANK] + terms, own[2 * RANK:3 * RANK]], 0)).astype(BF16))
-    db[...] = dot(jnp.concatenate(mids, 1), xb[...].reshape(2 * tokens, model))
-    for p in range(width // up_width):
-        up_copy(p).wait_recv()
-
-    down_block, up_block = model // frames, width // frames
-    rows = 3 * RANK
-    lane = lax.broadcasted_iota(jnp.int32, (rows, 128), 1)
-
-    def blocks_of(to):
-        wide = [db[:, pl.ds(pl.multiple_of(zz * X * down_block + to * 128, 128), 256)] for zz in range(Z)]
-        turned = [pltpu.roll(w, lax.rem(256 - 32 * to, 256), 1) for w in wide]
-        return turned
-
-    @pl.when(core == 1)
-    def _():
-        upb[:, 0:width] += upr[0:rows].astype(F32)
-
-    def left_half(to):
-        return jnp.concatenate([t[:, 0:128] for t in blocks_of(to)], 0)
-
-    def right_half(to):
-        out = []
-        for zz, turned in enumerate(blocks_of(to)):
-            start = zz * X * up_block + to * up_block
-            tile = pl.multiple_of(start // 128 * 128, 128)
-            third = upb[:, pl.ds(tile, 256)]
-            third = pltpu.roll(third, lax.rem(256 + 32 - start % 128, 256), 1)[:, 0:128]
-            out.append(jnp.where(lane < 32, turned[:, 128:256], jnp.where(lane < 32 + up_block, third, 0.0)))
-        return jnp.concatenate(out, 0)
+    both_mids = jnp.concatenate(mids, 1)
 
     x_copies = [remote(xsb.at[i], xrx.at[i], xs_sem.at[i], xr_sem.at[i], xs[i]) for i in range(X - 1)]
 
-    def send_half(half):
-        for i in (1, 0, 2):
-            xsb[i] = half((x + 1 + i) % X).astype(BF16)
-            x_copies[i].start()
-        st[...] = half(x)
-
-    @pl.when(core == 0)
-    def _():
-        send_half(left_half)
-
-    @pl.when(core == 1)
-    def _():
-        send_half(right_half)
-
+    def half_of(to):
+        wide = dot(both_mids, xp[to])
+        return jnp.concatenate([wide[:, zz * 128:(zz + 1) * 128] for zz in range(Z)], 0) + upl[to]
+
+    for i in (1, 0, 2):
+        xsb[i] = half_of((x + 1 + i) % X).astype(BF16)
+        x_copies[i].start()
+    st[...] = half_of(x)
     total = st[...]
     for i in range(X - 1):
         x_copies[i].wait_recv()
@@ -305,18 +304,23 @@
     last.start()
     last.wait_recv()
     left, right = fb[0], fb[1]
-    shifted = pltpu.roll(right, 128 - 32, 1)
-    for place, c in enumerate((1, 2, 0)):
-        part = slice(place * RANK, (place + 1) * RANK)
-        down_out[c, :, 0:128] = left[part]
-        down_out[c, :, 128:down_block] = right[part, 0:down_block - 128]
-        up_out[c] = shifted[part, 0:up_block]
+    out[:, 0:128] = left
+    out[:, 128:256] = right
     for p in range(width // up_width):
         up_copy(p).wait_send()
     for i in range(4):
         pl.when(can_send[i % 2])(mid_copies[i].wait_send)
     for copy in [input_copy, own_copy] + x_copies + z_copies + y_copies + [last]:
         copy.wait_send()
+
+
+def unpack(both, down_out, up_out):
+    down_block, up_block = down_out.shape[2], up_out.shape[2]
+    shifted = pltpu.roll(both[:, 128:256], 128 - 32, 1)
+    for place, c in enumerate((1, 2, 0)):
+        part = slice(place * RANK, (place + 1) * RANK)
+        down_out[c] = both[part, 0:down_block]
+        up_out[c] = shifted[part, 0:up_block]
 
 
 def per_device(frames, dps, q, k, v, g, x, blocks, a, u):
@@ -340,7 +344,7 @@
         vmem((3, 2 * RANK, tokens), BF16), vmem((2 * RANK, tokens), BF16), vmem((4 * RANK, width), BF16),
         vmem((tokens, width), BF16), vmem((3 * tokens, width), BF16), vmem((3 * tokens, width), BF16),
         vmem((3, rows, tokens), F32), vmem((2, 2, 2 * RANK, tokens), F32), vmem((rows, tokens), F32),
-        vmem((rows, model), F32), vmem((rows, width + 128), F32), vmem((4 * RANK, width), BF16), vmem((4 * RANK, width), BF16),
+        vmem((X, 2 * tokens, Z * 128), BF16), vmem((X, Z * rows, 128), F32), vmem((rows, width + 128), F32), vmem((4 * RANK, width), BF16), vmem((4 * RANK, width), BF16),
         vmem((Z * rows, 128), F32),
         vmem((X - 1, Z * rows, 128), BF16), vmem((X - 1, Z * rows, 128), BF16),
         vmem((Z, 32, 128), BF16), vmem((Z, rows, 128), F32), vmem((max(Z - 1, 1), 32, 128), BF16),
@@ -349,17 +353,23 @@
         dma((width // up_width,)), dma((width // up_width,)), dma, dma, dma((X - 1,)), dma((X - 1,)), dma((max(Z - 1, 1),)), dma((max(Z - 1, 1),)),
         dma((max(Y - 1, 1),)), dma((max(Y - 1, 1),)), dma, dma,
     ]
+    both = pl.pallas_call(
+        functools.partial(kernel, (frames, dps, chunks, chunk, window, up_width, lag)),
+        out_shape=jax.ShapeDtypeStruct((rows, 256), F32),
+        in_specs=[pl.BlockSpec(memory_space=pltpu.HBM)] * 8,
+        out_specs=pl.BlockSpec(memory_space=pltpu.VMEM),
+        scratch_shapes=scratch,
+        compiler_params=pltpu.CompilerParams(collective_id=0, has_side_effects=True, vmem_limit_bytes=60 << 20),
+    )(q, k, v, g, x, jnp.transpose(blocks, (1, 2, 3, 0)), a, u)
     return pl.pallas_call(
-        functools.partial(kernel, (frames, dps, chunks, chunk, window, up_width, lag)),
+        unpack,
         out_shape=(
             jax.ShapeDtypeStruct((3, RANK, model // frames), F32),
             jax.ShapeDtypeStruct((3, RANK, width // frames), F32),
         ),
-        in_specs=[pl.BlockSpec(memory_space=pltpu.HBM)] * 8,
+        in_specs=[pl.BlockSpec(memory_space=pltpu.VMEM)],
         out_specs=(pl.BlockSpec(memory_space=pltpu.VMEM), pl.BlockSpec(memory_space=pltpu.VMEM)),
-        scratch_shapes=scratch,
-        compiler_params=pltpu.CompilerParams(collective_id=0, has_side_effects=True, vmem_limit_bytes=60 << 20),
-    )(q, k, v, g, x, jnp.transpose(blocks, (1, 2, 3, 0)), a, u)
+    )(both)
 
 
 def solution(mesh):

time: 72.7 us -> 71.2 us (0.979)
  local copies, waits for them, and re-layouts: 2.65 us -> 0 us
  Pallas kernels: 69.1 us -> 70.3 us
    unnamed x2 -> x0, local copies, waits for them, and re-layouts: 2.65 us -> none
    pallas_call x0 -> x1, Pallas kernels: none -> 1.41 us  [per_device(): pl.pallas_call(unpack, out_shape=(jax.ShapeDtypeStruct((3, RANK, model //...]
where the time goes in v4:
time: 71.2 us; the launch traced here: 71 us
  Pallas kernels  70.3 us (99%)
    pallas_call x1, Pallas kernels, per_device(): pl.pallas_call(functools.partial(kernel, (frames, dps, chunks, chunk, win...  68.9 us

profile of v4, /device:TPU:1, one launch (start us, length us, event | category | flops | bytes accessed | tf_op | source)
XLA Modules:
  0.0 71.0 jit_solution(16110883647699700194)
XLA Ops:
  0.6 68.9 %shard_map.95.both = f32[24,256]{1,0:T(8,128)} custom-call(bf16[1,128,2560]{2,1,0:T(8,128)(2,1)} %q_hbm.1, bf16[1,128,2560]{2,1,0:T(8,128)(2,1)} %k_hbm.1, bf16[1,128,2560]{2,1,0:T(8,128)(2,1)} %v_hbm.1, bf16[1,128,2560]{2,1,0:T(8,128)(2,1)} %g_hbm.1, bf16[1,128,5120]{2,1,0:T(8,128)(2,1)} %x_hbm.1, s32[3,4,4,32]{3,2,1,0:T(4,128)} %bitcast.1, ...), custom_call_target="tpu_custom_call" | custom-call | tf_op jit(solution)/shard_map/pallas_call | solution.py:356
  69.6 1.4 %shard_map.96 = (f32[3,8,160]{2,1,0:T(8,128)}, f32[3,8,80]{2,1,0:T(8,128)}) custom-call(f32[24,256]{1,0:T(8,128)} %shard_map.95.both), custom_call_target="tpu_custom_call" | custom-call | tf_op jit(solution)/shard_map/pallas_call | solution.py:364

commit v5 on v4

--- a/solution.py
+++ b/solution.py
@@ -74,7 +74,7 @@
             (x_hbm.at[0], xb.at[0]), (a_hbm, ab), (u_hbm, ub), (blocks_hbm, bb),
         ])
     ]
-    for copy in local:
+    for copy in local[0:2]:
         copy.start()
     for side, (slot, absent) in enumerate(((0, frame == 0), (2, frame == frames - 1))):
         @pl.when(absent)
@@ -109,6 +109,9 @@
     @pl.loop(0, window)
     def _(c):
         halo_start(c)
+
+    for copy in local[2:]:
+        copy.start()
 
     local[7].wait()
     lane_block = lax.broadcasted_iota(jnp.int32, (4, tokens), 1) // (tokens // 4)
@@ -299,13 +302,13 @@
     total = yrx[0].astype(F32)
     for i in range(1, Y):
         total = total + yrx[i].astype(F32)
-    fb[core] = total[0:rows]
-    last = remote(fb.at[core], fb.at[core], fs_sem, fr_sem, sibling)
+    fb[...] = total[0:rows]
+    last = remote(fb, out.at[core], fs_sem, fr_sem, sibling)
     last.start()
+    here = pltpu.make_async_copy(fb, out.at[core], local_sem.at[0])
+    here.start()
+    here.wait()
     last.wait_recv()
-    left, right = fb[0], fb[1]
-    out[:, 0:128] = left
-    out[:, 128:256] = right
     for p in range(width // up_width):
         up_copy(p).wait_send()
     for i in range(4):
@@ -316,10 +319,12 @@
 
 def unpack(both, down_out, up_out):
     down_block, up_block = down_out.shape[2], up_out.shape[2]
-    shifted = pltpu.roll(both[:, 128:256], 128 - 32, 1)
+    left, right = both[0], both[1]
+    shifted = pltpu.roll(right, 128 - 32, 1)
     for place, c in enumerate((1, 2, 0)):
         part = slice(place * RANK, (place + 1) * RANK)
-        down_out[c] = both[part, 0:down_block]
+        down_out[c, :, 0:128] = left[part]
+        down_out[c, :, 128:down_block] = right[part, 0:down_block - 128]
         up_out[c] = shifted[part, 0:up_block]
 
 
@@ -348,16 +353,16 @@
         vmem((Z * rows, 128), F32),
         vmem((X - 1, Z * rows, 128), BF16), vmem((X - 1, Z * rows, 128), BF16),
         vmem((Z, 32, 128), BF16), vmem((Z, rows, 128), F32), vmem((max(Z - 1, 1), 32, 128), BF16),
-        vmem((32, 128), BF16), vmem((Y, 32, 128), BF16), vmem((2, rows, 128), F32),
+        vmem((32, 128), BF16), vmem((Y, 32, 128), BF16), vmem((rows, 128), F32),
         dma((8,)), dma((2, 2, chunks)), dma((2, 2, chunks)), dma((2,)), dma((2,)), dma((3, 2)), dma((3, 2)),
         dma((width // up_width,)), dma((width // up_width,)), dma, dma, dma((X - 1,)), dma((X - 1,)), dma((max(Z - 1, 1),)), dma((max(Z - 1, 1),)),
         dma((max(Y - 1, 1),)), dma((max(Y - 1, 1),)), dma, dma,
     ]
     both = pl.pallas_call(
         functools.partial(kernel, (frames, dps, chunks, chunk, window, up_width, lag)),
-        out_shape=jax.ShapeDtypeStruct((rows, 256), F32),
+        out_shape=jax.ShapeDtypeStruct((2, rows, 128), F32),
         in_specs=[pl.BlockSpec(memory_space=pltpu.HBM)] * 8,
-        out_specs=pl.BlockSpec(memory_space=pltpu.VMEM),
+        out_specs=pl.BlockSpec(memory_space=pl.ANY),
         scratch_shapes=scratch,
         compiler_params=pltpu.CompilerParams(collective_id=0, has_side_effects=True, vmem_limit_bytes=60 << 20),
     )(q, k, v, g, x, jnp.transpose(blocks, (1, 2, 3, 0)), a, u)

time: 71.2 us -> 70.7 us (level)
  no operation moved by 1% of the time
where the time goes in v5:
time: 70.7 us; the launch traced here: 70.5 us
  Pallas kernels  69.9 us (99%)
    pallas_call x1, Pallas kernels, per_device(): pl.pallas_call(functools.partial(kernel, (frames, dps, chunks, chunk, win...  68.5 us

profile of v5, /device:TPU:1, one launch (start us, length us, event | category | flops | bytes accessed | tf_op | source)
XLA Modules:
  0.0 70.5 jit_solution(17918346240910438445)
XLA Ops:
  0.6 68.5 %shard_map.95.both = f32[2,24,128]{2,1,0:T(8,128)} custom-call(bf16[1,128,2560]{2,1,0:T(8,128)(2,1)} %q_hbm.1, bf16[1,128,2560]{2,1,0:T(8,128)(2,1)} %k_hbm.1, bf16[1,128,2560]{2,1,0:T(8,128)(2,1)} %v_hbm.1, bf16[1,128,2560]{2,1,0:T(8,128)(2,1)} %g_hbm.1, bf16[1,128,5120]{2,1,0:T(8,128)(2,1)} %x_hbm.1, s32[3,4,4,32]{3,2,1,0:T(4,128)} %bitcast.1, ...), custom_call_target="tpu_custom_call" | custom-call | tf_op jit(solution)/shard_map/pallas_call | solution.py:361
  69.1 1.4 %shard_map.96 = (f32[3,8,160]{2,1,0:T(8,128)}, f32[3,8,80]{2,1,0:T(8,128)}) custom-call(f32[2,24,128]{2,1,0:T(8,128)} %shard_map.95.both), custom_call_target="tpu_custom_call" | custom-call | tf_op jit(solution)/shard_map/pallas_call | solution.py:369

commit v6 on v5

--- a/solution.py
+++ b/solution.py
@@ -179,11 +179,6 @@
     @pl.loop(0, chunks)
     def _(c):
         for side in range(2):
-            @pl.when(can_send[side])
-            def _():
-                for kind in range(2):
-                    halo_copy(c, side, kind).wait_send()
-
             @pl.when(can_recv[side])
             def _():
                 for kind in range(2):
@@ -309,6 +304,14 @@
     here.start()
     here.wait()
     last.wait_recv()
+    @pl.loop(0, chunks)
+    def _(c):
+        for side in range(2):
+            @pl.when(can_send[side])
+            def _():
+                for kind in range(2):
+                    halo_copy(c, side, kind).wait_send()
+
     for p in range(width // up_width):
         up_copy(p).wait_send()
     for i in range(4):

time: 70.7 us -> 70.8 us (level)
  no operation moved by 1% of the time
where the time goes in v6:
time: 70.8 us; the launch traced here: 70.6 us
  Pallas kernels  69.9 us (99%)
    pallas_call x1, Pallas kernels, per_device(): pl.pallas_call(functools.partial(kernel, (frames, dps, chunks, chunk, win...  68.5 us

profile of v6, /device:TPU:1, one launch (start us, length us, event | category | flops | bytes accessed | tf_op | source)
XLA Modules:
  0.0 70.6 jit_solution(9472868763808137099)
XLA Ops:
  0.6 68.5 %shard_map.95.both = f32[2,24,128]{2,1,0:T(8,128)} custom-call(bf16[1,128,2560]{2,1,0:T(8,128)(2,1)} %q_hbm.1, bf16[1,128,2560]{2,1,0:T(8,128)(2,1)} %k_hbm.1, bf16[1,128,2560]{2,1,0:T(8,128)(2,1)} %v_hbm.1, bf16[1,128,2560]{2,1,0:T(8,128)(2,1)} %g_hbm.1, bf16[1,128,5120]{2,1,0:T(8,128)(2,1)} %x_hbm.1, s32[3,4,4,32]{3,2,1,0:T(4,128)} %bitcast.1, ...), custom_call_target="tpu_custom_call" | custom-call | tf_op jit(solution)/shard_map/pallas_call | solution.py:364
  69.1 1.4 %shard_map.96 = (f32[3,8,160]{2,1,0:T(8,128)}, f32[3,8,80]{2,1,0:T(8,128)}) custom-call(f32[2,24,128]{2,1,0:T(8,128)} %shard_map.95.both), custom_call_target="tpu_custom_call" | custom-call | tf_op jit(solution)/shard_map/pallas_call | solution.py:372
